TPU v7x, 32 devices: a whole 2x2x4 slice. The times are simulated.
32 devices in a mesh: node: 2 (over x), row: 16 (over z, y, core).
Axes of the slice: x: 2, y: 2, z: 4, core: 2. Of those that a mesh axis runs over, the one named last changes fastest.
Arguments:
- hamiltonian: float32 [32, 7, 128, 128], P('row'), may hold values from -0.09375 to 0.09375
- column_blocks: int32 [32, 7], P('row'), may hold values from 0 to 31, as said below
- start_basis: float32 [4096, 256], P('row'), may hold values from -48 to 48
- node_re: float32 [6], P('node'), may hold values from 1.5 to 2.5
- node_im: float32 [6], P('node'), may hold values from 0.5 to 1.5
- weight_re: float32 [6], P('node'), may hold values from 0.5 to 1.5
- weight_im: float32 [6], P('node'), may hold values from -1 to 1
- sweep_count: int32 [6], P('node'), may hold values from 1 to 2, as said below
Outputs:
- basis: float32 [4096, 256], P('row')
Inputs may be any that keep to these rules, and one draw needn't show every extreme that they name: `column_blocks`: tile 0 of row block b lies in column block b, tile 1 in b - 2 and tile 2 in b + 2, taken cyclically modulo 32; every other tile lies within 2 blocks of b, cyclically. `sweep_count`: some node takes 1 sweep and some node takes 2.
All inputs are finite; a program needn't handle non-finite values.
Results may differ from a plain program's by a relative error of at most 0.00022.
Values sent between devices are 32-bit elements; how exact they have to be, the bound alone decides.
No kernel may reach another device: no remote copies, remote signals or barrier semaphores. Data moves between devices by JAX's collectives and lax.ppermute only.
A program may use at most 64 MiB of HBM per device.

v0:
```python
import math
import jax
import jax.numpy as jnp
from jax import lax
from jax.sharding import PartitionSpec as P

REACH = 2
SWEEPS = 2
NS_ITERS = 2


def extended_2(block, sides, width):
    for axis, dim in sides:
        count = lax.axis_size(axis)
        forward = [(i, i + 1) for i in range(count - 1)]
        forward.append((count - 1, 0))
        backward = [(target, source) for source, target in forward]
        low = lax.ppermute(
            lax.slice_in_dim(block, block.shape[dim] - width, None, axis=dim), axis, forward
        )
        high = lax.ppermute(lax.slice_in_dim(block, 0, width, axis=dim), axis, backward)
        block = jnp.concatenate([low, block, high], axis=dim)
    return block


def apply_local(hamiltonian, local_cols, extended):
    breadth = extended.shape[1]
    count_blocks = hamiltonian.shape[0]
    tile_rows = hamiltonian.shape[2]
    blocks = extended.reshape(-1, tile_rows, breadth)
    summed = jnp.zeros((count_blocks, tile_rows, breadth), jnp.float32)
    for column in range(hamiltonian.shape[1]):
        picked = jnp.take(blocks, local_cols[:, column], axis=0)
        summed = summed + jnp.einsum(
            "bij,bjw->biw", hamiltonian[:, column], picked, precision=lax.Precision.HIGHEST
        )
    return summed.reshape(count_blocks * tile_rows, breadth)


def local_gram(vectors):
    return lax.dot_general(
        vectors, vectors, (((0,), (0,)), ((), ())), precision=lax.Precision.HIGHEST
    )


def orthonormal(gram_matrix):
    norm_value = jnp.sqrt(jnp.sum(gram_matrix * gram_matrix) + 1e-06)
    matrix_a = gram_matrix / norm_value
    identity = jnp.eye(gram_matrix.shape[0], dtype=jnp.float32)
    current = identity
    for repeat in range(NS_ITERS):
        middle = 1.5 * identity - 0.5 * jnp.dot(current, matrix_a, precision=lax.Precision.HIGHEST)
        matrix_a = jnp.dot(matrix_a, middle, precision=lax.Precision.HIGHEST)
        current = jnp.dot(middle, current, precision=lax.Precision.HIGHEST)
    return (current, norm_value)


def finish(vectors, gram_matrix, row_scale):
    mixing, norm_value = orthonormal(gram_matrix)
    return (
        row_scale * jnp.dot(vectors, mixing, precision=lax.Precision.HIGHEST) / jnp.sqrt(norm_value)
    )


def on_device(
    hamiltonian, column_blocks, start_basis, node_re, node_im, weight_re, weight_im, sweep_count
):
    count_blocks = hamiltonian.shape[0]
    tile_rows = hamiltonian.shape[2]
    devices_row = lax.axis_size("row")
    first_block = lax.axis_index("row") * count_blocks
    local_cols = (column_blocks - first_block + REACH + count_blocks * devices_row) % (
        count_blocks * devices_row
    )
    rim_rows = REACH * tile_rows
    row_scale = math.sqrt(start_basis.shape[0] * devices_row)
    modulus = node_re * node_re + node_im * node_im
    inverse_re = node_re / modulus
    inverse_im = -node_im / modulus
    power_re, power_im = (inverse_re, inverse_im)
    listed = []
    for degree in range(SWEEPS + 1):
        active = (sweep_count >= degree).astype(jnp.float32)
        listed.append(jnp.sum(active * (weight_re * power_re - weight_im * power_im)))
        power_re, power_im = (
            power_re * inverse_re - power_im * inverse_im,
            power_re * inverse_im + power_im * inverse_re,
        )
    coefficients = lax.psum(jnp.stack(listed), "node")
    krylov = start_basis
    filtered = coefficients[0] * start_basis
    for degree in range(1, SWEEPS + 1):
        extended = extended_2(krylov, (("row", 0),), rim_rows)
        krylov = apply_local(hamiltonian, local_cols, extended)
        filtered = filtered + coefficients[degree] * krylov
    gram_matrix = lax.psum(local_gram(filtered), "row")
    return finish(filtered, gram_matrix, row_scale)


def solution(mesh):
    return jax.shard_map(
        on_device,
        mesh=mesh,
        in_specs=(
            P("row", None, None, None),
            P("row", None),
            P("row", None),
            P("node"),
            P("node"),
            P("node"),
            P("node"),
            P("node"),
        ),
        out_specs=P("row", None),
        check_vma=False,
    )
```

profile of v0, /device:TPU:1, one launch (start us, length us, event | category | flops | bytes accessed | tf_op | source)
XLA Modules:
  0.0 155.2 jit_solution(14468664168108451764)
XLA Ops:
  6.5 2.6 %collective-permute-start = (f32[256,256]{1,0:T(8,128)}, f32[256,256]{1,0:T(8,128)S(1)}, u32[]{:S(2)}, u32[]{:S(2)}) collective-permute-start(f32[256,256]{1,0:T(8,128)} %param.12), channel_id=1, source_target_pairs={{0,1},{1,2},{2,3},{3,4},{4,5},{5,6},{6,7},{7,8},{8,9},{9,10},{10,1... | collective-permute-start | bytes 786440 | tf_op jit(solution)/shard_map/ppermute | solution.py:18
  9.2 0.7 copy-done.20
  10.7 0.6 compare_and_fusion.4
  14.9 3.1 %collective-permute-done.1 = f32[256,256]{1,0:T(8,128)S(1)} collective-permute-done((f32[256,256]{1,0:T(8,128)}, f32[256,256]{1,0:T(8,128)S(1)}, u32[]{:S(2)}, u32[]{:S(2)}) %collective-permute-start.1) | collective-permute-done | bytes 262176 | tf_op jit(solution)/shard_map/ppermute | solution.py:21
  18.0 1.0 pad_maximum_fusion
  21.9 0.7 gather_fusion.5
  22.6 0.7 gather_fusion.6
  23.3 1.1 fusion.18
  25.4 0.7 copy-done.5
  26.6 0.6 copy-done.11
  27.7 0.7 copy-done.7
  31.4 0.6 fusion.79
  32.0 1.9 %pad_maximum_fusion.2 = f32[3]{0:T(128)S(1)} fusion(f32[1]{0:T(128)} %bitcast.2, f32[1]{0:T(128)} %bitcast.1, f32[1]{0:T(128)} %bitcast), kind=kLoop, calls=%fused_computation.151 | loop fusion | flops 6 | bytes 24 | tf_op jit(solution)/shard_map/stack | solution.py:89
  33.9 4.1 %psum.14 = f32[3]{0:T(128)S(1)} all-reduce(f32[3]{0:T(128)S(1)} %pad_maximum_fusion.2), channel_id=1, replica_groups=mesh['node'=2,'row'=16] {'node'}, use_global_device_ids=true, to_apply=%region_3.4 | all-reduce | flops 3 | bytes 24 | tf_op jit(solution)/shard_map/psum | solution.py:89
  38.0 0.6 fusion.97
  41.2 0.7 gather_fusion.11
  41.9 0.7 gather_fusion.12
  42.6 1.4 gather_fusion.13
  48.4 1.1 fusion.3
  49.5 1.3 bitcast_add_fusion
  50.8 1.3 fusion.98
  52.1 91.0 %all-reduce.2.cloned.1.call-done = f32[256,256]{1,0:T(8,128)} async-done(((f32[256,256]{1,0:T(8,128)}), f32[256,256]{1,0:T(8,128)}) %all-reduce.2.cloned.1.call-update) | async-done | bytes 262160 | tf_op jit(solution)/shard_map/psum | solution.py:96
  143.1 1.7 %multiply_reduce_fusion = f32[]{:T(128)} fusion(f32[256,256]{1,0:T(8,128)} %all-reduce.2.cloned.1.call-done), kind=kLoop, calls=%fused_computation.52 | loop fusion | flops 131071 | bytes 262148 | tf_op jit(solution)/shard_map/reduce_sum | solution.py:47
  147.3 1.1 fusion
  (101 shorter events, 20.8 us)
Async XLA Ops:
  6.5 136.6 %all-reduce.2.cloned.1.call-start = ((), (), s32[]{:S(2)}) async-start(), calls=%async_computation | async-start | bytes 524288 | tf_op jit(solution)/shard_map/psum | solution.py:96
  6.5 8.3 %collective-permute-start = (f32[256,256]{1,0:T(8,128)}, f32[256,256]{1,0:T(8,128)S(1)}, u32[]{:S(2)}, u32[]{:S(2)}) collective-permute-start(f32[256,256]{1,0:T(8,128)} %param.12), channel_id=1, source_target_pairs={{0,1},{1,2},{2,3},{3,4},{4,5},{5,6},{6,7},{7,8},{8,9},{9,10},{10,1... | collective-permute-start | bytes 786440 | tf_op jit(solution)/shard_map/ppermute | solution.py:18
  9.2 8.8 %collective-permute-start.1 = (f32[256,256]{1,0:T(8,128)}, f32[256,256]{1,0:T(8,128)S(1)}, u32[]{:S(2)}, u32[]{:S(2)}) collective-permute-start(f32[256,256]{1,0:T(8,128)} %param.12), channel_id=1, source_target_pairs={{1,0},{2,1},{3,2},{4,3},{5,4},{6,5},{7,6},{8,7},{9,8},{10,9},{11,1... | collective-permute-start | bytes 786440 | tf_op jit(solution)/shard_map/ppermute | solution.py:21
  9.2 0.7 copy-start.20
  13.1 8.2 %copy-start.4 = (s32[1024]{0:T(1024)}, s32[1024]{0:T(1024)S(1)}, u32[]{:S(2)}) copy-start(s32[1024]{0:T(1024)S(1)} %pad_clamp_fusion.2) | copy-start | bytes 12292
  13.7 0.7 copy-start.21
  13.7 0.7 copy-start.22
  21.3 2.0 %copy-start = (f32[2,7,128,128]{3,2,1,0:T(8,128)S(1)}, f32[2,7,128,128]{3,2,1,0:T(8,128)}, u32[]{:S(2)}) copy-start(f32[2,7,128,128]{3,2,1,0:T(8,128)} %param.10) | copy-start | bytes 2752516
  25.4 0.7 copy-start.5
  26.6 0.7 copy-start.11
  27.7 0.7 copy-start.7
  29.0 0.7 copy-start.15
  29.7 1.0 copy-start.24
  29.7 1.1 copy-start.25
  30.1 8.5 %collective-permute-start.2 = (f32[256,256]{1,0:T(8,128)S(1)}, f32[256,256]{1,0:T(8,128)S(1)}, u32[]{:S(2)}, u32[]{:S(2)}) collective-permute-start(f32[256,256]{1,0:T(8,128)S(1)} %bitcast.89), channel_id=1, source_target_pairs={{0,1},{1,2},{2,3},{3,4},{4,5},{5,6},{6,7},{7,8},{8,9},{9,10},{10,1... | collective-permute-start | bytes 786440 | tf_op jit(solution)/shard_map/ppermute | solution.py:18
  30.2 8.7 %collective-permute-start.3 = (f32[256,256]{1,0:T(8,128)S(1)}, f32[256,256]{1,0:T(8,128)S(1)}, u32[]{:S(2)}, u32[]{:S(2)}) collective-permute-start(f32[256,256]{1,0:T(8,128)S(1)} %bitcast.90), channel_id=1, source_target_pairs={{1,0},{2,1},{3,2},{4,3},{5,4},{6,5},{7,6},{8,7},{9,8},{10,9},{11,1... | collective-permute-start | bytes 786440 | tf_op jit(solution)/shard_map/ppermute | solution.py:21
  30.7 0.7 copy-start.23
  42.6 1.4 copy-start.19
  44.6 0.7 copy-start.6
  45.9 0.7 copy-start.8
  47.2 0.9 copy-start.2
  47.7 0.7 copy-start.16
  48.4 1.1 copy-start.1
  143.1 2.4 %copy-start.3 = (f32[256,256]{1,0:T(8,128)S(1)}, f32[256,256]{1,0:T(8,128)}, u32[]{:S(2)}) copy-start(f32[256,256]{1,0:T(8,128)} %all-reduce.2.cloned.1.call-done) | copy-start | bytes 786436
  (7 other events, 4.3 us)
Sparse Core Ops, SparseCore 0:
  52.2 90.7 all-reduce.1
where the time goes:
time: 156 us; the launch traced here: 155 us
  waiting for transfers between devices  94.3 us (60%)
  local copies, waits for them, and re-layouts  16 us (10%)
  between operations  14.6 us (9%)
  matrix products  11.9 us (8%)
  other arithmetic  11.2 us (7%)
  blocking collectives  4.06 us (3%)
  starting transfers between devices  3.19 us (2%)
    psum x1, waiting for transfers between devices, on_device(): gram_matrix = lax.psum(local_gram(filtered), 'row')  91 us
    gather x14, local copies, waits for them, and re-layouts, apply_local(): picked = jnp.take(blocks, local_cols[:, column], axis=0)  9.23 us
    dot_general x14, matrix products, apply_local(): jnp.einsum('bij,bjw->biw', hamiltonian[:, column], picked, precision=lax....  7.73 us
    unnamed x52, local copies, waits for them, and re-layouts  5.86 us
    psum x1, blocking collectives, on_device(): coefficients = lax.psum(jnp.stack(listed), 'node')  4.06 us
    ppermute x2, waiting for transfers between devices, extended_2(): lax.ppermute(lax.slice_in_dim(block, 0, width, axis=dim), axis, backward)  3.36 us
  transfers between devices with their start and end apart: 5, of which 3 were waited for; matrix products, arithmetic and copies ran while one was open for 5% of the time, Pallas kernels for 0%

commit v1 on v0

--- a/solution.py
+++ b/solution.py
@@ -93,7 +93,7 @@
         extended = extended_2(krylov, (("row", 0),), rim_rows)
         krylov = apply_local(hamiltonian, local_cols, extended)
         filtered = filtered + coefficients[degree] * krylov
-    gram_matrix = lax.psum(local_gram(filtered), "row")
+    gram_matrix = jnp.sum(lax.all_gather(local_gram(filtered), "row"), axis=0)
     return finish(filtered, gram_matrix, row_scale)
 
 

time: 156 us -> 122 us (0.78)
  waiting for transfers between devices: 94.3 us -> 56.4 us
  matrix products: 11.9 us -> 19 us
  local copies, waits for them, and re-layouts: 16 us -> 9.99 us
  other arithmetic: 11.2 us -> 13 us
    psum x1 -> x0, waiting for transfers between devices: 91 us -> none  [on_device(): gram_matrix = lax.psum(local_gram(filtered), 'row')]
    all_gather x0 -> x1, waiting for transfers between devices: none -> 52.8 us  [on_device(): gram_matrix = jnp.sum(lax.all_gather(local_gram(filtered), 'row'), axis=0)]
    dot_general x14, matrix products: 7.73 us -> 14.8 us  [apply_local(): jnp.einsum('bij,bjw->biw', hamiltonian[:, column], picked, precision=lax....]
    unnamed x52 -> x26, local copies, waits for them, and re-layouts: 5.86 us -> 0.07 us
    reduce_sum x0 -> x1, other arithmetic: none -> 2.48 us  [on_device(): gram_matrix = jnp.sum(lax.all_gather(local_gram(filtered), 'row'), axis=0)]
    ppermute x2, starting transfers between devices: 2.69 us -> 4.36 us  [extended_2(): lax.ppermute(lax.slice_in_dim(block, block.shape[dim] - width, None, axis...]
  transfers between devices with their start and end apart: 5 -> 5, of which waited for: 3 -> 2; matrix products, arithmetic and copies ran while one was open for 5% -> 7% of each run, Pallas kernels for 0% -> 0%
where the time goes in v1:
time: 122 us; the launch traced here: 121 us
  waiting for transfers between devices  56.4 us (46%)
  matrix products  19 us (16%)
  between operations  14.6 us (12%)
  other arithmetic  13 us (11%)
  local copies, waits for them, and re-layouts  9.99 us (8%)
  starting transfers between devices  4.42 us (4%)
  blocking collectives  4.06 us (3%)
    all_gather x1, waiting for transfers between devices, on_device(): gram_matrix = jnp.sum(lax.all_gather(local_gram(filtered), 'row'), axis=0)  52.8 us
    dot_general x14, matrix products, apply_local(): jnp.einsum('bij,bjw->biw', hamiltonian[:, column], picked, precision=lax....  14.8 us
    gather x14, local copies, waits for them, and re-layouts, apply_local(): picked = jnp.take(blocks, local_cols[:, column], axis=0)  8.98 us
    ppermute x2, starting transfers between devices, extended_2(): lax.ppermute(lax.slice_in_dim(block, block.shape[dim] - width, None, axis...  4.36 us
    psum x1, blocking collectives, on_device(): coefficients = lax.psum(jnp.stack(listed), 'node')  4.06 us
    ppermute x2, waiting for transfers between devices, extended_2(): lax.ppermute(lax.slice_in_dim(block, 0, width, axis=dim), axis, backward)  3.6 us
    and x5, other arithmetic, apply_local(): picked = jnp.take(blocks, local_cols[:, column], axis=0)  2.85 us
    reduce_sum x1, other arithmetic, on_device(): gram_matrix = jnp.sum(lax.all_gather(local_gram(filtered), 'row'), axis=0)  2.48 us
  transfers between devices with their start and end apart: 5, of which 2 were waited for; matrix products, arithmetic and copies ran while one was open for 7% of the time, Pallas kernels for 0%

profile of v1, /device:TPU:1, one launch (start us, length us, event | category | flops | bytes accessed | tf_op | source)
XLA Modules:
  0.0 121.5 jit_solution(4901674898355003)
XLA Ops:
  6.5 2.6 %collective-permute-start = (f32[256,256]{1,0:T(8,128)}, f32[256,256]{1,0:T(8,128)S(1)}, u32[]{:S(2)}, u32[]{:S(2)}) collective-permute-start(f32[256,256]{1,0:T(8,128)} %param.12), channel_id=1, source_target_pairs={{0,1},{1,2},{2,3},{3,4},{4,5},{5,6},{6,7},{7,8},{8,9},{9,10},{10,1... | collective-permute-start | bytes 786440 | tf_op jit(solution)/shard_map/ppermute | solution.py:18
  13.1 1.2 %fusion.82 = (f32[3]{0:T(128)}, f32[3]{0:T(128)}) fusion(f32[3]{0:T(128)} %param.13, f32[3]{0:T(128)} %param.14), kind=kLoop, calls=%fused_computation.156 | loop fusion | flops 18 | bytes 48 | tf_op jit(solution)/shard_map/div | solution.py:78
  14.4 3.6 %collective-permute-done.1 = f32[256,256]{1,0:T(8,128)S(1)} collective-permute-done((f32[256,256]{1,0:T(8,128)}, f32[256,256]{1,0:T(8,128)S(1)}, u32[]{:S(2)}, u32[]{:S(2)}) %collective-permute-start.1) | collective-permute-done | bytes 262176 | tf_op jit(solution)/shard_map/ppermute | solution.py:21
  23.1 1.2 fusion.18
  24.3 1.1 convolution_add_fusion.11
  25.4 1.1 convolution_add_fusion.10
  26.5 1.1 convolution_add_fusion.9
  27.6 1.1 convolution_add_fusion.8
  29.7 1.7 %collective-permute-start.2 = (f32[256,256]{1,0:T(8,128)S(1)}, f32[256,256]{1,0:T(8,128)S(1)}, u32[]{:S(2)}, u32[]{:S(2)}) collective-permute-start(f32[256,256]{1,0:T(8,128)S(1)} %bitcast.92), channel_id=1, source_target_pairs={{0,1},{1,2},{2,3},{3,4},{4,5},{5,6},{6,7},{7,8},{8,9},{9,10},{10,1... | collective-permute-start | bytes 786440 | tf_op jit(solution)/shard_map/ppermute | solution.py:18
  32.1 2.0 %pad_maximum_fusion.2 = f32[3]{0:T(128)S(1)} fusion(f32[1]{0:T(128)} %bitcast.2, f32[1]{0:T(128)} %bitcast.1, f32[1]{0:T(128)} %bitcast), kind=kLoop, calls=%fused_computation.151 | loop fusion | flops 6 | bytes 24 | tf_op jit(solution)/shard_map/stack | solution.py:89
  34.1 4.1 %psum.7 = f32[3]{0:T(128)S(1)} all-reduce(f32[3]{0:T(128)S(1)} %pad_maximum_fusion.2), channel_id=1, replica_groups=mesh['node'=2,'row'=16] {'node'}, use_global_device_ids=true, to_apply=%region_3.4 | all-reduce | flops 3 | bytes 24 | tf_op jit(solution)/shard_map/psum | solution.py:89
  38.9 1.4 %gather_fusion.13 = f32[2,128,256]{2,1,0:T(8,128)} fusion(f32[6,128,256]{2,1,0:T(8,128)S(1)} %bitcast.76, s32[1024]{0:T(1024)} %copy-done.3), kind=kCustom, calls=%fused_computation.13.clone | custom fusion | bytes 524296 | tf_op jit(solution)/shard_map/jit(_take)/gather | solution.py:33
  44.0 1.2 fusion.10
  45.2 1.1 convolution_add_fusion.5
  46.3 1.1 convolution_add_fusion.4
  47.4 1.1 convolution_add_fusion.3
  48.5 1.1 convolution_add_fusion.2
  49.5 1.1 convolution_add_fusion.1
  50.7 1.8 %fusion.3 = f32[2,256,128]{1,2,0:T(8,128)S(1)} fusion(f32[2,256,128]{1,2,0:T(8,128)S(1)} %convolution_add_fusion.1, f32[2,128,256]{2,1,0:T(8,128)S(1)} %copy-done.2, f32[]{:T(128)} %bitcast.15, pred[2]{0:T(512)(128)(4,1)} %compare_and_fusion, f32[2,7,128,128]{3,2,1,0:T(8,128)S(1)} %copy-done), kind=kOutput, calls=%fused_computation.21 | convolution fusion | flops 100859904 | bytes 917510 | tf_op jit(solution)/shard_map/bij,bjw->biw/dot_general | solution.py:34
  52.5 1.3 %bitcast_add_fusion = f32[256,256]{1,0:T(8,128)S(1)} fusion(f32[2,256,128]{1,2,0:T(8,128)S(1)} %fusion.3, f32[256,256]{1,0:T(8,128)S(1)} %copy-done.1, f32[]{:T(128)} %bitcast.4, f32[]{:T(128)} %bitcast.3, f32[2,256,128]{1,2,0:T(8,128)S(1)} %convolution_add_fusion.6), kind=kLoop, calls=%fused_computation.35 | loop fusion | flops 262144 | bytes 1048584 | tf_op jit(solution)/shard_map/add | solution.py:95
  53.8 1.3 %fusion.98 = f32[256,256]{1,0:T(8,128)} fusion(f32[256,256]{1,0:T(8,128)S(1)} %bitcast_add_fusion), kind=kOutput, calls=%fused_computation.172 | convolution fusion | flops 201326592 | bytes 524288 | tf_op jit(solution)/shard_map/dot_general | solution.py:41
  55.1 52.8 %all-gather.3.cloned.1.call-done = f32[4096,256]{1,0:T(8,128)} async-done(((f32[256,256]{1,0:T(8,128)}), f32[4096,256]{1,0:T(8,128)}) %all-gather.3.cloned.1.call-update) | async-done | bytes 4194320 | tf_op jit(solution)/shard_map/all_gather | solution.py:96
  107.9 2.5 %reduce_sum.48 = f32[256,256]{1,0:T(8,128)S(1)} reduce(f32[16,256,256]{2,1,0:T(8,128)} %bitcast.90, f32[]{:T(128)} %constant.22.clone.1), dimensions={0}, to_apply=%region_4.6 | reduce | flops 983040 | bytes 4456452 | tf_op jit(solution)/shard_map/reduce_sum | solution.py:96
  113.5 1.1 fusion
  (76 shorter events, 17.3 us)
Async XLA Ops:
  6.5 16.5 %copy-start = (f32[2,7,128,128]{3,2,1,0:T(8,128)S(1)}, f32[2,7,128,128]{3,2,1,0:T(8,128)}, u32[]{:S(2)}) copy-start(f32[2,7,128,128]{3,2,1,0:T(8,128)} %param.10) | copy-start | bytes 2752516
  6.5 101.4 %all-gather.3.cloned.1.call-start = ((), (), s32[]{:S(2)}) async-start(), calls=%async_computation | async-start | bytes 4456448 | tf_op jit(solution)/shard_map/all_gather | solution.py:96
  6.5 7.9 %collective-permute-start = (f32[256,256]{1,0:T(8,128)}, f32[256,256]{1,0:T(8,128)S(1)}, u32[]{:S(2)}, u32[]{:S(2)}) collective-permute-start(f32[256,256]{1,0:T(8,128)} %param.12), channel_id=1, source_target_pairs={{0,1},{1,2},{2,3},{3,4},{4,5},{5,6},{6,7},{7,8},{8,9},{9,10},{10,1... | collective-permute-start | bytes 786440 | tf_op jit(solution)/shard_map/ppermute | solution.py:18
  9.2 8.8 %collective-permute-start.1 = (f32[256,256]{1,0:T(8,128)}, f32[256,256]{1,0:T(8,128)S(1)}, u32[]{:S(2)}, u32[]{:S(2)}) collective-permute-start(f32[256,256]{1,0:T(8,128)} %param.12), channel_id=1, source_target_pairs={{1,0},{2,1},{3,2},{4,3},{5,4},{6,5},{7,6},{8,7},{9,8},{10,9},{11,1... | collective-permute-start | bytes 786440 | tf_op jit(solution)/shard_map/ppermute | solution.py:21
  13.1 6.5 %copy-start.3 = (s32[1024]{0:T(1024)}, s32[1024]{0:T(1024)S(1)}, u32[]{:S(2)}) copy-start(s32[1024]{0:T(1024)S(1)} %pad_clamp_fusion) | copy-start | bytes 12292
  13.1 7.6 %copy-start.4 = (s32[1024]{0:T(1024)}, s32[1024]{0:T(1024)S(1)}, u32[]{:S(2)}) copy-start(s32[1024]{0:T(1024)S(1)} %pad_clamp_fusion.3) | copy-start | bytes 12292
  13.1 6.4 %copy-start.5 = (s32[1024]{0:T(1024)}, s32[1024]{0:T(1024)S(1)}, u32[]{:S(2)}) copy-start(s32[1024]{0:T(1024)S(1)} %pad_clamp_fusion.1) | copy-start | bytes 12292
  23.0 5.6 %copy-start.7 = (pred[2]{0:T(512)(128)(4,1)S(1)}, pred[2]{0:T(512)(128)(4,1)}, u32[]{:S(2)}) copy-start(pred[2]{0:T(512)(128)(4,1)} %compare_and_fusion.1) | copy-start | bytes 10
  23.1 6.1 %copy-start.6 = (pred[2]{0:T(512)(128)(4,1)S(1)}, pred[2]{0:T(512)(128)(4,1)}, u32[]{:S(2)}) copy-start(pred[2]{0:T(512)(128)(4,1)} %compare_and_fusion) | copy-start | bytes 10
  23.1 8.4 %copy-start.8 = (f32[3]{0:T(128)S(1)}, f32[3]{0:T(128)}, u32[]{:S(2)}) copy-start(f32[3]{0:T(128)} %get-tuple-element.16) | copy-start | bytes 40
  23.1 8.4 %copy-start.9 = (f32[3]{0:T(128)S(1)}, f32[3]{0:T(128)}, u32[]{:S(2)}) copy-start(f32[3]{0:T(128)} %get-tuple-element.17) | copy-start | bytes 40
  23.1 8.3 %copy-start.10 = (s32[3]{0:T(128)S(1)}, s32[3]{0:T(128)}, u32[]{:S(2)}) copy-start(s32[3]{0:T(128)} %param.17) | copy-start | bytes 40
  23.1 8.3 %copy-start.11 = (f32[3]{0:T(128)S(1)}, f32[3]{0:T(128)}, u32[]{:S(2)}) copy-start(f32[3]{0:T(128)} %param.16) | copy-start | bytes 40
  23.1 8.3 %copy-start.12 = (f32[3]{0:T(128)S(1)}, f32[3]{0:T(128)}, u32[]{:S(2)}) copy-start(f32[3]{0:T(128)} %param.15) | copy-start | bytes 40
  29.6 9.2 %collective-permute-start.3 = (f32[256,256]{1,0:T(8,128)S(1)}, f32[256,256]{1,0:T(8,128)S(1)}, u32[]{:S(2)}, u32[]{:S(2)}) collective-permute-start(f32[256,256]{1,0:T(8,128)S(1)} %bitcast.91), channel_id=1, source_target_pairs={{1,0},{2,1},{3,2},{4,3},{5,4},{6,5},{7,6},{8,7},{9,8},{10,9},{11,1... | collective-permute-start | bytes 786440 | tf_op jit(solution)/shard_map/ppermute | solution.py:21
  29.7 9.1 %collective-permute-start.2 = (f32[256,256]{1,0:T(8,128)S(1)}, f32[256,256]{1,0:T(8,128)S(1)}, u32[]{:S(2)}, u32[]{:S(2)}) collective-permute-start(f32[256,256]{1,0:T(8,128)S(1)} %bitcast.92), channel_id=1, source_target_pairs={{0,1},{1,2},{2,3},{3,4},{4,5},{5,6},{6,7},{7,8},{8,9},{9,10},{10,1... | collective-permute-start | bytes 786440 | tf_op jit(solution)/shard_map/ppermute | solution.py:18
  43.9 6.7 %copy-start.2 = (f32[2,128,256]{2,1,0:T(8,128)S(1)}, f32[2,128,256]{2,1,0:T(8,128)}, u32[]{:S(2)}) copy-start(f32[2,128,256]{2,1,0:T(8,128)} %gather_fusion.13) | copy-start | bytes 786436
  44.0 8.5 %copy-start.1 = (f32[256,256]{1,0:T(8,128)S(1)}, f32[256,256]{1,0:T(8,128)}, u32[]{:S(2)}) copy-start(f32[256,256]{1,0:T(8,128)} %param.12) | copy-start | bytes 786436
Sparse Core Ops, SparseCore 0:
  55.2 52.6 all-gather.2
